TPU v7x, 128 devices: a whole 4x4x4 slice. The times are simulated.
128 devices in a mesh: tm: 16 (over y, z_hi, core), state: 8 (over z_lo, x).
Axes of the slice: x: 4, y: 4, z: 4 (z_hi: 2, z_lo: 2; z = z_hi * 2 + z_lo), core: 2. Of those that a mesh axis runs over, the one named last changes fastest.
Arguments:
- spikes: int32 [2304, 32768], P(None, 'tm'), may hold values from 0 to 3
- log_rate: bfloat16 [32768, 4096], P('tm', 'state'), may hold values from -0.03125 to 0.03125
- forward: bfloat16 [2304, 4096], P('tm', 'state'), may hold values from 0.019897461 to 1
- backward: float32 [2304, 4096], P('tm', 'state'), may hold values from 0.1 to 10
- transition: bfloat16 [4096, 4096], P(None, 'state'), may hold values from 0.049804688 to 1
- rate_total: float32 [4096], P('state'), may hold values from 0 to 3
- edge_weight: float32 [4096], P('state'), may hold values from 0.1 to 10
- block_mask: int32 [32, 32], replicated, may hold values 0 or 1
Outputs:
- transition_counts: float32 [4096, 4096], P('tm', 'state')
- pair_loglik: float32 [2304], P('tm')
All inputs are finite; a program needn't handle non-finite values.
Results may differ from a plain program's by a relative error of at most 0.0005.
Values may be sent and summed in bfloat16 or wider, within the bound.
A program may use at most 128 MiB of HBM per device.

v0:
```python
import jax
import jax.numpy as jnp
from jax import lax
from jax.sharding import PartitionSpec as P

STATES = 4096
BLOCK = 128


def shifted(value, axis, steps):
    count = lax.axis_size(axis)
    initial, last = (max(0, -steps), min(count, count - steps))
    return lax.ppermute(value, axis, [(source, source + steps) for source in range(initial, last)])


def shards(spikes, log_rate, forward, backward, transition, rate_total, edge_weight, block_mask):
    dest_width = transition.shape[1]
    time_total = spikes.shape[0]
    tm_count = lax.axis_size("tm")
    tm_position = lax.axis_index("tm")
    state_position = lax.axis_index("state")
    rows_out = STATES // tm_count
    spike_rows = spikes.astype(log_rate.dtype)
    drive_sum = lax.psum_scatter(
        jnp.dot(spike_rows, log_rate, preferred_element_type=jnp.float32),
        "tm",
        scatter_dimension=0,
        tiled=True,
    )
    right_term = jnp.exp(drive_sum - rate_total[None, :]) * backward
    boundary = shifted(right_term[:1], "tm", -1)
    boundary = jnp.where(tm_position == tm_count - 1, edge_weight[None, :], boundary)
    ahead_bins = jnp.concatenate([right_term[1:], boundary], axis=0)
    gathered = lax.all_gather(forward, "state", axis=1, tiled=True)
    blocks = block_mask.shape[0]
    allowed = jnp.maximum(block_mask, jnp.eye(blocks, dtype=jnp.int32))
    mask_columns = jnp.repeat(allowed, BLOCK, axis=1)
    mask_columns = lax.dynamic_slice_in_dim(
        mask_columns, state_position * dest_width, dest_width, 1
    )
    mask_full = jnp.repeat(mask_columns, BLOCK, axis=0)
    allowed_moves = transition * mask_full.astype(transition.dtype)
    carried = jnp.dot(gathered, allowed_moves, preferred_element_type=jnp.float32)
    totals = lax.psum(jnp.sum(carried * ahead_bins, axis=1), "state")
    pair_loglik = jnp.log(totals)
    weights = (ahead_bins / totals[:, None]).astype(forward.dtype)
    pair_sums = lax.psum_scatter(
        lax.dot_general(
            gathered, weights, (((0,), (0,)), ((), ())), preferred_element_type=jnp.float32
        ),
        "tm",
        scatter_dimension=0,
        tiled=True,
    )
    moves_here = lax.dynamic_slice_in_dim(allowed_moves, tm_position * rows_out, rows_out, 0)
    count_scale = STATES * STATES / time_total
    transition_counts = moves_here.astype(jnp.float32) * pair_sums * count_scale
    return (transition_counts, pair_loglik)


def solution(mesh):
    in_specs = (
        P(None, "tm"),
        P("tm", "state"),
        P("tm", "state"),
        P("tm", "state"),
        P(None, "state"),
        P("state"),
        P("state"),
        P(),
    )
    out_specs = (P("tm", "state"), P("tm"))
    return jax.shard_map(shards, mesh=mesh, in_specs=in_specs, out_specs=out_specs, check_vma=False)
```

profile of v0, /device:TPU:1, one launch (start us, length us, event | category | flops | bytes accessed | tf_op | source)
XLA Modules:
  0.0 255.2 jit_solution(17528824084718267944)
XLA Ops:
  8.0 0.0 copy-start
  8.0 0.0 reduce-scatter.3.cloned.1.call-start
  8.1 1.5 copy-done
  9.6 11.1 %fusion = f32[2304,512]{1,0:T(8,128)} fusion(bf16[2048,512]{1,0:T(8,128)(2,1)S(1)} %copy-done, s32[2304,2048]{1,0:T(8,128)} %param.8), kind=kOutput, calls=%fused_computation | convolution fusion | flops 4836556800 | bytes 25690112 | tf_op jit(solution)/shard_map/dot_general | solution.py:25
  20.7 0.0 reduce-scatter.3.cloned.1.call-update
  20.7 0.0 all-gather.2.cloned.1.call-start
  20.8 0.5 all-gather.2.cloned.1.call-update
  21.3 0.0 reduce-scatter.5.cloned.1.call-start
  21.4 0.1 copy-done.4
  21.4 0.1 copy.10
  21.5 6.4 %copy.11 = bf16[4096,512]{0,1:T(8,128)(2,1)} copy(bf16[4096,512]{1,0:T(8,128)(2,1)} %param.12) | data formatting | bytes 8388608 | tf_op args[4]
  27.9 0.1 broadcast_in_dim.11
  28.1 77.8 %reduce-scatter.3.cloned.1.call-done = f32[144,512]{1,0:T(8,128)} async-done(((f32[2304,512]{1,0:T(8,128)}), f32[144,512]{1,0:T(8,128)}) %reduce-scatter.3.cloned.1.call-update) | async-done | bytes 294928 | tf_op jit(solution)/shard_map/reduce_scatter | solution.py:24
  105.9 0.0 copy-done.3
  105.9 0.0 copy-done.5
  105.9 1.2 exponential_multiply_fusion
  107.1 3.9 %collective-permute-start = (f32[1,512]{1,0:T(1,128)S(1)}, f32[1,512]{1,0:T(1,128)S(1)}, u32[]{:S(2)}, u32[]{:S(2)}) collective-permute-start(f32[1,512]{1,0:T(1,128)S(1)} %slice.9), channel_id=1, source_target_pairs={{8,0},{16,8},{24,16},{32,24},{40,32},{48,40},{56,48},{64,56},{72,6... | collective-permute-start | bytes 6152 | tf_op jit(solution)/shard_map/ppermute | solution.py:13
  111.0 3.7 %broadcast_in_dim.12 = bf16[32,128,512]{1,0,2:T(8,128)(2,1)S(1)} broadcast(bf16[32,512]{0,1:T(8,128)(2,1)S(1)} %dynamic-slice_convert_fusion), dimensions={0,2} | broadcast | bytes 4227072 | tf_op jit(solution)/shard_map/broadcast_in_dim | solution.py:41
  114.7 0.0 copy-done.1
  114.7 0.0 copy-start.6
  114.7 3.3 %bitcast_multiply_fusion = bf16[4096,512]{0,1:T(8,128)(2,1)} fusion(bf16[4096,512]{0,1:T(8,128)(2,1)S(1)} %copy-done.1, bf16[64,8,32,128]{3,2,1,0:T(8,128)(2,1)S(1)} %bitcast.19), kind=kLoop, calls=%fused_computation.3 | loop fusion | flops 2097152 | bytes 12582912 | tf_op jit(solution)/shard_map/mul | solution.py:42
  118.1 0.7 slice.8
  118.8 0.0 collective-permute-done
  118.8 0.0 all-gather.2.cloned.1.call-done
  118.9 4.3 %fusion.3 = f32[144]{0:T(256)S(1)} fusion(bf16[4096,512]{0,1:T(8,128)(2,1)} %bitcast_multiply_fusion, bf16[144,4096]{1,0:T(8,128)(2,1)} %all-gather.2.cloned.1.call-done, f32[1,512]{1,0:T(1,128)S(1)} %broadcast_select_fusion, f32[143,512]{1,0:T(8,128)} %slice.8), kind=kOutput, calls=%fused_computation.6 | convolution fusion | flops 604200832 | bytes 5669440 | tf_op jit(solution)/shard_map/dot_general | solution.py:43
  123.2 15.1 %psum.7 = f32[144]{0:T(256)S(1)} all-reduce(f32[144]{0:T(256)S(1)} %fusion.3), channel_id=1, replica_groups=mesh['tm'=16,'state'=8] {'state'}, use_global_device_ids=true, to_apply=%region_2.3 | all-reduce | flops 144 | bytes 1152 | tf_op jit(solution)/shard_map/psum | solution.py:44
  138.3 5.6 %convolution_bitcast_fusion = f32[4096,512]{0,1:T(8,128)} fusion(bf16[144,4096]{1,0:T(8,128)(2,1)S(1)} %copy-done.2, f32[1,512]{1,0:T(1,128)S(1)} %broadcast_select_fusion, f32[143,512]{1,0:T(8,128)} %slice.8, f32[144]{0:T(256)S(1)} %psum.7), kind=kOutput, calls=%fused_computation.2 | convolution fusion | flops 604200960 | bytes 9863744 | tf_op jit(solution)/shard_map/dot_general | solution.py:48
  143.9 0.0 reduce-scatter.5.cloned.1.call-update
  143.9 0.6 log.3
  144.5 101.1 %reduce-scatter.5.cloned.1.call-done = f32[256,512]{0,1:T(8,128)} async-done(((f32[4096,512]{0,1:T(8,128)}), f32[256,512]{0,1:T(8,128)}) %reduce-scatter.5.cloned.1.call-update) | async-done | bytes 524304 | tf_op jit(solution)/shard_map/reduce_scatter | solution.py:47
  245.6 1.2 multiply_multiply_fusion
  246.8 1.0 copy.12
  (11 shorter events, 0.1 us)
Async XLA Ops:
  8.0 1.6 copy-start
  8.0 97.9 %reduce-scatter.3.cloned.1.call-start = ((), (), s32[]{:S(2)}) async-start(), calls=%async_computation.2 | async-start | bytes 5013504 | tf_op jit(solution)/shard_map/reduce_scatter | solution.py:24
  20.7 0.7 copy-start.4
  20.7 98.1 %all-gather.2.cloned.1.call-start = ((), (), s32[]{:S(2)}) async-start(), calls=%async_computation.3 | async-start | bytes 1327104 | tf_op jit(solution)/shard_map/all_gather | solution.py:34
  21.3 224.3 %reduce-scatter.5.cloned.1.call-start = ((), (), s32[]{:S(2)}) async-start(), calls=%async_computation.4 | async-start | bytes 8912896 | tf_op jit(solution)/shard_map/reduce_scatter | solution.py:47
  21.5 84.4 %copy-start.3 = (f32[144,512]{1,0:T(8,128)S(1)}, f32[144,512]{1,0:T(8,128)}, u32[]{:S(2)}) copy-start(f32[144,512]{1,0:T(8,128)} %param.11) | copy-start | bytes 884740
  21.5 84.4 %copy-start.5 = (f32[512]{0:T(512)S(1)}, f32[512]{0:T(512)}, u32[]{:S(2)}) copy-start(f32[512]{0:T(512)} %param.13) | copy-start | bytes 6148
  105.9 8.8 %copy-start.1 = (bf16[4096,512]{0,1:T(8,128)(2,1)S(1)}, bf16[4096,512]{0,1:T(8,128)(2,1)}, u32[]{:S(2)}) copy-start(bf16[4096,512]{0,1:T(8,128)(2,1)} %copy.11) | copy-start | bytes 12582916
  107.1 11.7 %collective-permute-start = (f32[1,512]{1,0:T(1,128)S(1)}, f32[1,512]{1,0:T(1,128)S(1)}, u32[]{:S(2)}, u32[]{:S(2)}) collective-permute-start(f32[1,512]{1,0:T(1,128)S(1)} %slice.9), channel_id=1, source_target_pairs={{8,0},{16,8},{24,16},{32,24},{40,32},{48,40},{56,48},{64,56},{72,6... | collective-permute-start | bytes 6152 | tf_op jit(solution)/shard_map/ppermute | solution.py:13
  114.7 4.1 %copy-start.6 = (f32[512]{0:T(512)S(1)}, f32[512]{0:T(512)}, u32[]{:S(2)}) copy-start(f32[512]{0:T(512)} %param.14) | copy-start | bytes 6148
  118.9 19.4 %copy-start.2 = (bf16[144,4096]{1,0:T(8,128)(2,1)S(1)}, bf16[144,4096]{1,0:T(8,128)(2,1)}, u32[]{:S(2)}) copy-start(bf16[144,4096]{1,0:T(8,128)(2,1)} %all-gather.2.cloned.1.call-done) | copy-start | bytes 3538948
Sparse Core Ops, SparseCore 0:
  20.8 84.9 reduce-scatter.2
  144.0 101.5 reduce-scatter.4
Sparse Core Ops, SparseCore 1:
  22.9 37.5 all-gather.1
where the time goes:
time: 256 us; the launch traced here: 255 us
  waiting for transfers between devices  179 us (70%)
  matrix products  21 us (8%)
  between operations  15.6 us (6%)
  blocking collectives  15.1 us (6%)
  local copies, waits for them, and re-layouts  14.3 us (6%)
  other arithmetic  5.71 us (2%)
  starting transfers between devices  4.06 us (2%)
    reduce_scatter x1, waiting for transfers between devices, shards(): lax.psum_scatter(lax.dot_general(gathered, weights, (((0,), (0,)), ((), (...  101 us
    reduce_scatter x1, waiting for transfers between devices, shards(): lax.psum_scatter(jnp.dot(spike_rows, log_rate, preferred_element_type=jnp...  77.8 us
    psum x1, blocking collectives, shards(): totals = lax.psum(jnp.sum(carried * ahead_bins, axis=1), 'state')  15.1 us
    dot_general x1, matrix products, shards(): jnp.dot(spike_rows, log_rate, preferred_element_type=jnp.float32)  11.1 us
    unnamed x16, local copies, waits for them, and re-layouts  9.05 us
    dot_general x1, matrix products, shards(): lax.dot_general(gathered, weights, (((0,), (0,)), ((), ())), preferred_el...  5.56 us
  transfers between devices with their start and end apart: 4, of which 2 were waited for; matrix products, arithmetic and copies ran while one was open for 6% of the time, Pallas kernels for 0%

commit v1 on v0

v1 whole, which is shorter than its diff:
```python
import functools
import jax
import jax.numpy as jnp
from jax import lax
from jax.experimental import pallas as pl
from jax.experimental.pallas import tpu as pltpu
from jax.sharding import PartitionSpec as P

MESH = pl.DeviceIdType.MESH
STATES = 4096
BLOCK = 128
F32, BF16, I16 = jnp.float32, jnp.bfloat16, jnp.int16
TOP = 32760.0
ROUND = 12582912.0
STEPS = ((2, 1), (1, 1), (3, 1), (0, 1), (2, 0), (1, 0), (3, 0), (0, 0))
YS = (2, 1, 3)


def encode(value):
    most = jnp.maximum(jnp.max(jnp.abs(value), axis=0, keepdims=True), 1e-30)
    coded = (value * (TOP / most) + ROUND) - ROUND
    return coded.astype(jnp.int32).astype(I16), jnp.broadcast_to(most * (1.0 / TOP), (8, value.shape[1]))


def decode(coded, scale):
    return coded.astype(jnp.int32).astype(F32) * scale[0:1, :]


def kernel(time_total, spikes, log_rate, forward, backward, transition, rate, edge, mask,
           counts, loglik,
           spk, lr, fw, bw, tr, am, rt, ew, out,
           tail, fg, fr, cs, cr, acc,
           p1s, p1r, p1sc, p1rc, q1s, q1r, q1sc, q1rc, q2s, q2r, q2sc, q2rc, p2s, p2r, p2sc, p2rc,
           car, tcol, tot, tsum, first, w,
           lsem, ssem, csem, tailsem, f1sem, f2sem, f3sem, p1sem, q1sem, q2sem, p2sem, totsem, firstsem, wsem, coresem):
    tm, st = lax.axis_index("tm"), lax.axis_index("state")
    y, zh, c = tm // 4, (tm // 2) % 2, tm % 2
    zl, x = st // 4, st % 4

    def at(dy=0, dz=0, dc=0):
        return (((y + dy) % 4) * 2 + (zh + dz) % 2) * 2 + (c + dc) % 2

    def sat(dx=0, dl=0):
        return ((zl + dl) % 2) * 4 + (x + dx) % 4

    rows = fw.shape[0]
    group = 2 * rows
    half = 256

    def local(src, dst, i):
        cp = pltpu.make_async_copy(src, dst, lsem.at[i])
        cp.start()
        return cp

    def spike_load(s):
        dy, dz = STEPS[s]
        row = pl.multiple_of((((y + dy) % 4) * 2 + (zh + dz) % 2) * group, group)
        return local(spikes.at[pl.ds(row, group), :], spk.at[s % spk.shape[0]], s % spk.shape[0])

    loads = {}
    load_fw = local(forward, fw, 4)
    load_lr = local(log_rate, lr, 5)
    for s in range(spk.shape[0]):
        loads[s] = spike_load(s)
    load_tr = local(transition, tr, 6)
    load_bw = local(backward, bw, 7)
    load_rt = local(rate, rt, 8)
    load_ew = local(edge, ew, 9)

    barrier = pltpu.get_barrier_semaphore()
    prev, nxt = (tm + 15) % 16, (tm + 1) % 16
    peers = [(at(dc=1), st)] + [(at(dy, dz, dc), st) for dy in range(4) for dz in range(2) for dc in range(2) if (dy, dz) != (0, 0)]
    peers += [(tm, sat(dx, dl)) for dx in range(4) for dl in range(2) if (dx, dl) != (0, 0)]
    for peer in peers:
        pl.semaphore_signal(barrier, inc=1, device_id=peer, device_id_type=MESH)
    pl.semaphore_wait(barrier, len(peers))

    sends = []

    def send(src, dst, rsem, device):
        i = len(sends)
        cp = pltpu.make_async_remote_copy(src, dst, ssem.at[i], rsem, device_id=device, device_id_type=MESH)
        cp.start()
        sends.append(cp)
        return cp

    def arrive(dst, rsem):
        pltpu.make_async_remote_copy(dst, dst, ssem.at[0], rsem, device_id=(tm, st), device_id_type=MESH).wait_recv()

    load_fw.wait()
    send(fw.at[pl.ds(rows - 16, 16), :], tail, tailsem.at[0], (nxt, st))
    load_lr.wait()

    def drive(s):
        loads[s].wait()
        part = jnp.dot(spk[s % spk.shape[0]].astype(F32).astype(BF16), lr[...], preferred_element_type=F32)
        parts = part.reshape(2, rows, 512)
        acc[s] = jnp.where(c == 0, parts[0], parts[1])
        cs[s] = jnp.where(c == 0, parts[1], parts[0])
        send(cs.at[s], cr.at[s], csem.at[s], (at(dc=1), st))
        if s + spk.shape[0] < 8:
            loads[s + spk.shape[0]] = spike_load(s + spk.shape[0])

    def pair_up(s):
        dy, dz = STEPS[s]
        arrive(cr.at[s], csem.at[s])
        if dy != 0:
            i = dz * 3 + dy - 1
            p1s[i], p1sc[i] = encode(acc[s, :, 0:half] + cr[s, :, 0:half])
            to = (at(dy), st)
            send(p1s.at[i], p1r.at[i], p1sem.at[0, i], to)
            send(p1sc.at[i], p1rc.at[i], p1sem.at[1, i], to)
        else:
            acc[s, :, 0:half] += cr[s, :, 0:half]
        if dz != 0:
            q1s[dy], q1sc[dy] = encode(acc[s, :, half:] + cr[s, :, half:])
            to = (at(0, 1), st)
            send(q1s.at[dy], q1r.at[dy], q1sem.at[0, dy], to)
            send(q1sc.at[dy], q1rc.at[dy], q1sem.at[1, dy], to)
        else:
            acc[s, :, half:] += cr[s, :, half:]

    def q_second(s):
        dy, _ = STEPS[s]
        arrive(q1r.at[dy], q1sem.at[0, dy])
        arrive(q1rc.at[dy], q1sem.at[1, dy])
        value = acc[s, :, half:] + decode(q1r[dy], q1rc[dy])
        if dy == 0:
            acc[s, :, half:] = value
        else:
            i = dy - 1
            q2s[i], q2sc[i] = encode(value)
            to = (at(dy), st)
            send(q2s.at[i], q2r.at[i], q2sem.at[0, i], to)
            send(q2sc.at[i], q2rc.at[i], q2sem.at[1, i], to)

    def p_sum(s):
        dz = STEPS[s][1]
        value = acc[s, :, 0:half]
        for dy in YS:
            i = dz * 3 + dy - 1
            arrive(p1r.at[i], p1sem.at[0, i])
            arrive(p1rc.at[i], p1sem.at[1, i])
            value = value + decode(p1r[i], p1rc[i])
        return value

    drive(0)
    arrive(tail, tailsem.at[0])
    turned = pltpu.roll(fw[...].astype(F32), 1, 0)
    above = jnp.broadcast_to(tail[...].astype(F32)[15:16, :], (rows, 512))
    at_top = lax.broadcasted_iota(jnp.int32, (rows, 512), 0) == 0
    fg[st] = jnp.where(at_top, above, turned).astype(BF16)
    send(fg.at[st], fg.at[st], f1sem.at[st], (tm, sat(0, 1)))
    for dx in (1, 3, 2):
        send(fg.at[st], fg.at[st], f1sem.at[st], (tm, sat(dx)))
    for s in range(1, 8):
        drive(s)
        pair_up(s - 1)
        if s == 2:
            other = sat(0, 1)
            arrive(fg.at[other], f1sem.at[other])
            for dx in (1, 3, 2):
                send(fg.at[other], fg.at[other], f1sem.at[other], (tm, sat(dx)))
        if s >= 6:
            q_second(s - 2)
    pair_up(7)
    q_second(6)
    value = p_sum(3)
    p2s[0], p2sc[0] = encode(value)
    to = (at(0, 1), st)
    send(p2s.at[0], p2r.at[0], p2sem.at[0], to)
    send(p2sc.at[0], p2rc.at[0], p2sem.at[1], to)
    q_second(7)

    load_tr.wait()

    @pl.loop(0, STATES // BLOCK)
    def _(ib):
        for cb in range(4):
            jb = st * 4 + cb
            keep = jnp.maximum(mask[ib, jb], (ib == jb).astype(jnp.int32)).astype(F32)
            at_rows = pl.ds(pl.multiple_of(ib * BLOCK, BLOCK), BLOCK)
            at_cols = pl.ds(cb * BLOCK, BLOCK)
            am[at_rows, at_cols] = (tr[at_rows, at_cols].astype(F32) * keep).astype(BF16)

    for dl in (0, 1):
        for dx in (1, 3, 2):
            who = sat(dx, dl)
            arrive(fg.at[who], f1sem.at[who])
    owner = x // 2
    quarter = x % 2
    mine = c == owner
    qcols = pl.ds(pl.multiple_of(x * 128, 128), 128)
    f2 = []
    for dy, dz in STEPS:
        i = len(sends)
        to_group = ((y + dy) % 4) * 2 + (zh + dz) % 2
        src = fg.at[to_group, :, qcols]
        dst = fr.at[quarter, tm]
        cp = pltpu.make_async_remote_copy(src, dst, ssem.at[i], f2sem.at[tm], device_id=(to_group * 2 + owner, st), device_id_type=MESH)
        sends.append(cp)
        if (dy, dz) != (0, 0):
            cp.start()
        else:
            own_cp = pltpu.make_async_copy(src, dst, f2sem.at[tm])
            pl.when(mine)(own_cp.start)
            pl.when(jnp.logical_not(mine))(cp.start)
            sends.pop()
            last_f2 = cp
            sends.append(None)
    car[...] = jnp.zeros_like(car)
    for b in range(8):
        car[...] += jnp.dot(fg[b], am[pl.ds(b * 512, 512), :], preferred_element_type=F32)

    load_bw.wait()
    load_rt.wait()
    load_ew.wait()
    value = p_sum(7)
    arrive(p2r.at[0], p2sem.at[0])
    arrive(p2rc.at[0], p2sem.at[1])
    p_drive = value + decode(p2r[0], p2rc[0])
    q_drive = acc[7, :, half:]
    for dy in YS:
        i = dy - 1
        arrive(q2r.at[i], q2sem.at[0, i])
        arrive(q2rc.at[i], q2sem.at[1, i])
        q_drive = q_drive + decode(q2r[i], q2rc[i])
    is_edge = jnp.logical_and(lax.broadcasted_iota(jnp.int32, (rows, half), 0) == 0, tm == 0)
    ahead = []
    total = jnp.zeros((rows, 1), F32)
    for h, drive_sum in enumerate((p_drive, q_drive)):
        cols = slice(h * half, (h + 1) * half)
        term = jnp.exp(drive_sum - rt[:, cols]) * bw[:, cols]
        term = jnp.where(is_edge, jnp.broadcast_to(ew[:, cols], (rows, half)), term)
        acc[0, :, cols] = term
        total = total + jnp.sum(term * car[:, cols], axis=1, keepdims=True)
    tcol[pl.ds(0, rows), :] = jnp.broadcast_to(total, (rows, 128))
    tcol[pl.ds(rows, 256 - rows), :] = jnp.ones((256 - rows, 128), F32)
    tot[st] = tcol[...].T[0:8, :]
    for dx, dl in ((2, 1), (2, 0), (1, 1), (3, 1), (1, 0), (3, 0), (0, 1)):
        send(tot.at[st], tot.at[st], totsem.at[st], (tm, sat(dx, dl)))

    @pl.when(mine)
    def _():
        pltpu.make_async_copy(fr.at[quarter, tm], fr.at[quarter, tm], f2sem.at[tm]).wait()
        for dy, dz in STEPS:
            for dc in range(2):
                if (dy, dz, dc) != (0, 0, 0):
                    arrive(fr.at[quarter, at(dy, dz, dc)], f2sem.at[at(dy, dz, dc)])
        for dx in (1, 3, 2):
            pltpu.make_async_remote_copy(fr.at[quarter], fr.at[quarter], f3sem.at[0, dx], f3sem.at[1, quarter],
                                         device_id=(tm, sat(dx)), device_id_type=MESH).start()

    for dx in range(4):
        for dl in range(2):
            if (dx, dl) != (0, 0):
                who = sat(dx, dl)
                arrive(tot.at[who], totsem.at[who])
    sums = tot[0]
    for b in range(1, 8):
        sums = sums + tot[b]
    tsum[...] = sums
    tcol[...] = jnp.broadcast_to(sums[0:1, :], (128, 256)).T
    norm = tcol[pl.ds(0, rows), :]
    for h in range(2):
        for q in range(2):
            cols = pl.ds(h * half + q * 128, 128)
            w[h, tm, :, pl.ds(q * 128, 128)] = (acc[0, :, cols] / norm).astype(BF16)

    def w_send(h, who, dy, dz, dc=0):
        send(w.at[h, who], w.at[h, who], (coresem if dc else wsem).at[h, who], (at(dy, dz, dc), st))

    def w_arrive(h, who, dc=0):
        arrive(w.at[h, who], (coresem if dc else wsem).at[h, who])

    w_send(0, tm, 0, 1)
    for dy in YS:
        w_send(1, tm, dy, 0)
    for dy in YS:
        w_send(0, tm, dy, 0)
    w_send(1, tm, 0, 1)
    w_send(0, tm, 0, 0, 1)
    w_send(1, tm, 0, 0, 1)
    send(tsum, first, firstsem.at[0], (prev, st))
    opp = at(0, 1)
    w_arrive(0, opp)
    for dy in YS:
        w_send(0, opp, dy, 0)
    w_send(0, opp, 0, 0, 1)
    for dy in (1, 3, 2):
        who = at(dy, 0)
        w_arrive(1, who)
        w_send(1, who, 0, 1)
        w_send(1, who, 0, 0, 1)
    for dy in (1, 3, 2):
        who = at(dy, 0)
        w_arrive(0, who)
        w_send(0, who, 0, 0, 1)
    w_arrive(1, opp)
    w_send(1, opp, 0, 0, 1)
    for dy in (1, 3, 2):
        for h in (0, 1):
            who = at(dy, 1)
            w_arrive(h, who)
            w_send(h, who, 0, 0, 1)

    arrive(first, firstsem.at[0])
    lanes = lax.broadcasted_iota(jnp.int32, (8, 256), 1)
    here = pltpu.roll(tsum[...], 255, 1)
    there = jnp.broadcast_to(first[...][:, 0:1], (8, 256))
    loglik[...] = jnp.log(jnp.where(lanes == rows - 1, there, here))

    for q in range(2):
        @pl.when(jnp.logical_not(jnp.logical_and(mine, quarter == q)))
        def _(q=q):
            pltpu.make_async_remote_copy(fr.at[q], fr.at[q], f3sem.at[0, 0], f3sem.at[1, q], device_id=(tm, st), device_id_type=MESH).wait_recv()
    for dy, dz in STEPS:
        for h in (0, 1):
            w_arrive(h, at(dy, dz, 1), 1)

    scale = STATES * STATES / time_total
    for h in range(2):
        right = w[h].reshape(16 * rows, half)
        for q in range(2):
            left = fr[q].reshape(16 * rows, 128)
            pair = lax.dot_general(left, right, (((0,), (0,)), ((), ())), preferred_element_type=F32)
            at_rows = pl.ds(pl.multiple_of(tm * 256 + q * 128, 128), 128)
            moves = am[at_rows, pl.ds(h * half, half)].astype(F32)
            out[pl.ds(q * 128, 128), pl.ds(h * half, half)] = moves * pair * scale
    store = local(out, counts, 10)

    for i, cp in enumerate(sends):
        if cp is not None:
            cp.wait_send()
    pl.when(jnp.logical_not(mine))(last_f2.wait_send)

    @pl.when(mine)
    def _():
        for dx in (1, 3, 2):
            pltpu.make_async_remote_copy(fr.at[quarter], fr.at[quarter], f3sem.at[0, dx], f3sem.at[1, quarter],
                                         device_id=(tm, sat(dx)), device_id_type=MESH).wait_send()
    store.wait()


def shards(spikes, log_rate, forward, backward, transition, rate_total, edge_weight, block_mask):
    rows = forward.shape[0]
    time_total = spikes.shape[0]
    neurons, width = log_rate.shape
    vm = pltpu.VMEM
    dma = pltpu.SemaphoreType.DMA
    scratch = [
        vm((3, 2 * rows, neurons), jnp.int32), vm((neurons, width), BF16), vm((rows, width), BF16), vm((rows, width), F32),
        vm((STATES, width), BF16), vm((STATES, width), BF16), vm((1, width), F32), vm((1, width), F32), vm((256, width), F32),
        vm((16, width), BF16), vm((8, rows, width), BF16), vm((2, 16, rows, 128), BF16),
        vm((8, rows, width), F32), vm((8, rows, width), F32), vm((8, rows, width), F32),
    ]
    for n in (6, 4, 3, 1):
        scratch += [vm((n, rows, 256), I16), vm((n, rows, 256), I16), vm((n, 8, 256), F32), vm((n, 8, 256), F32)]
    scratch += [
        vm((rows, width), F32), vm((256, 128), F32), vm((8, 8, 256), F32), vm((8, 256), F32), vm((8, 256), F32), vm((2, 16, rows, 256), BF16),
        dma((11,)), dma((120,)), dma((8,)), dma((1,)), dma((8,)), dma((16,)), dma((2, 4)), dma((2, 6)), dma((2, 4)), dma((2, 3)), dma((2,)),
        dma((8,)), dma((1,)), dma((2, 16)), dma((2, 16)),
    ]
    hbm = pl.BlockSpec(memory_space=pl.ANY)
    counts, loglik = pl.pallas_call(
        functools.partial(kernel, time_total),
        out_shape=(jax.ShapeDtypeStruct((256, width), F32), jax.ShapeDtypeStruct((8, 256), F32)),
        in_specs=[hbm] * 7 + [pl.BlockSpec(memory_space=pltpu.SMEM)],
        out_specs=(hbm, pl.BlockSpec(memory_space=pltpu.VMEM)),
        scratch_shapes=scratch,
        compiler_params=pltpu.CompilerParams(collective_id=0, has_side_effects=True, vmem_limit_bytes=56 * 2**20),
    )(spikes, log_rate, forward, backward, transition, rate_total.reshape(1, width), edge_weight.reshape(1, width), block_mask)
    return counts, loglik[0, :rows]


def solution(mesh):
    in_specs = (P(None, "tm"), P("tm", "state"), P("tm", "state"), P("tm", "state"), P(None, "state"), P("state"), P("state"), P())
    out_specs = (P("tm", "state"), P("tm"))
    return jax.shard_map(shards, mesh=mesh, in_specs=in_specs, out_specs=out_specs, check_vma=False)
```

time: 256 us -> 57.8 us (0.23)
  waiting for transfers between devices: 179 us -> 0 us
  Pallas kernels: 0 us -> 53.8 us
  matrix products: 21 us -> 0 us
  blocking collectives: 15.1 us -> 0 us
  between operations: 15.6 us -> 0.64 us
  local copies, waits for them, and re-layouts: 14.3 us -> 3.13 us
  other arithmetic: 5.71 us -> 0 us
  starting transfers between devices: 4.06 us -> 0 us
    reduce_scatter x2 -> x0, waiting for transfers between devices: 179 us -> none  [the longest x1 101 us: shards(): lax.psum_scatter(lax.dot_general(gathered, weights, (((0,), (0,)), ((), (...]
    pallas_call x0 -> x1, Pallas kernels: none -> 53.8 us  [shards(): pl.pallas_call(functools.partial(kernel, time_total), out_shape=(jax.Shap...]
    dot_general x3 -> x0, matrix products: 21 us -> none  [the longest x1 11.1 us: shards(): jnp.dot(spike_rows, log_rate, preferred_element_type=jnp.float32)]
    psum x1 -> x0, blocking collectives: 15.1 us -> none  [shards(): totals = lax.psum(jnp.sum(carried * ahead_bins, axis=1), 'state')]
    unnamed x16 -> x1, local copies, waits for them, and re-layouts: 9.05 us -> 1.87 us
    mul x3 -> x0, other arithmetic: 5.67 us -> none  [the longest x1 3.34 us: shards(): allowed_moves = transition * mask_full.astype(transition.dtype)]
    ppermute x1 -> x0, starting transfers between devices: 3.93 us -> none  [shifted(): lax.ppermute(value, axis, [(source, source + steps) for source in range(i...]
    broadcast_in_dim x2 -> x0, local copies, waits for them, and re-layouts: 3.82 us -> none  [the longest x1 3.69 us: shards(): mask_full = jnp.repeat(mask_columns, BLOCK, axis=0)]
  transfers between devices with their start and end apart: 4 -> 0, of which waited for: 2 -> 0; matrix products, arithmetic and copies ran while one was open for 6% -> 0% of each run, Pallas kernels for 0% -> 0%
where the time goes in v1:
time: 57.8 us; the launch traced here: 57.6 us
  Pallas kernels  53.8 us (93%)
  local copies, waits for them, and re-layouts  3.13 us (5%)
  between operations  0.64 us (1%)
    pallas_call x1, Pallas kernels, shards(): pl.pallas_call(functools.partial(kernel, time_total), out_shape=(jax.Shap...  53.8 us
    unnamed x1, local copies, waits for them, and re-layouts  1.87 us
    slice x1, local copies, waits for them, and re-layouts, shards(): return (counts, loglik[0, :rows])  1.26 us

profile of v1, /device:TPU:1, one launch (start us, length us, event | category | flops | bytes accessed | tf_op | source)
XLA Modules:
  0.0 57.6 jit_solution(981700973113495498)
XLA Ops:
  0.6 53.8 %shard_map.95 = (f32[256,512]{1,0:T(8,128)}, f32[8,256]{1,0:T(8,128)}) custom-call(s32[2304,2048]{1,0:T(8,128)} %spikes.1, bf16[2048,512]{1,0:T(8,128)(2,1)} %log_rate.1, bf16[144,512]{1,0:T(8,128)(2,1)} %forward.1, f32[144,512]{1,0:T(8,128)} %backward.1, bf16[4096,512]{1,0:T(8,128)(2,1)} %transition.1, f32[1,512]{1,0:T(1,128)} %bitcast.3, ...), custom_call_target="tpu_custom_call" | custom-call | tf_op jit(solution)/shard_map/pallas_call | solution.py:365
  54.4 1.3 %slice.3 = f32[1,144]{1,0:T(1,128)} slice(f32[8,256]{1,0:T(8,128)} %get-tuple-element.5), slice={[0:1], [0:144]} | slice | bytes 1152 | tf_op jit(solution)/shard_map/slice | solution.py:373
  55.7 1.9 %copy.11 = f32[256,512]{1,0:T(8,128)} copy(f32[256,512]{1,0:T(8,128)} %get-tuple-element.8) | data formatting | bytes 1048576

commit v2 on v1

--- a/solution.py
+++ b/solution.py
@@ -14,6 +14,8 @@
 ROUND = 12582912.0
 STEPS = ((2, 1), (1, 1), (3, 1), (0, 1), (2, 0), (1, 0), (3, 0), (0, 0))
 YS = (2, 1, 3)
+EARLY = 3
+RELAY = 4
 
 
 def encode(value):
@@ -26,9 +28,9 @@
     return coded.astype(jnp.int32).astype(F32) * scale[0:1, :]
 
 
-def kernel(time_total, spikes, log_rate, forward, backward, transition, rate, edge, mask,
+def kernel(time_total, spikes, log_rate, forward, backward, transition, rate, edge, block_mask,
            counts, loglik,
-           spk, lr, fw, bw, tr, am, rt, ew, out,
+           mask, lt, spk, lr, fw, bw, tr, am, rt, ew, out,
            tail, fg, fr, cs, cr, acc,
            p1s, p1r, p1sc, p1rc, q1s, q1r, q1sc, q1rc, q2s, q2r, q2sc, q2rc, p2s, p2r, p2sc, p2rc,
            car, tcol, tot, tsum, first, w,
@@ -58,22 +60,22 @@
         return local(spikes.at[pl.ds(row, group), :], spk.at[s % spk.shape[0]], s % spk.shape[0])
 
     loads = {}
-    load_fw = local(forward, fw, 4)
-    load_lr = local(log_rate, lr, 5)
+    load_fw = local(forward, fw, 8)
+    load_lr = local(log_rate, lr, 9)
     for s in range(spk.shape[0]):
         loads[s] = spike_load(s)
-    load_tr = local(transition, tr, 6)
-    load_bw = local(backward, bw, 7)
-    load_rt = local(rate, rt, 8)
-    load_ew = local(edge, ew, 9)
+    load_tr = local(transition, tr, 10)
+    load_mask = local(block_mask, mask, 15)
+    load_bw = local(backward, bw, 11)
+    load_rt = local(rate, rt, 12)
+    load_ew = local(edge, ew, 13)
 
     barrier = pltpu.get_barrier_semaphore()
     prev, nxt = (tm + 15) % 16, (tm + 1) % 16
-    peers = [(at(dc=1), st)] + [(at(dy, dz, dc), st) for dy in range(4) for dz in range(2) for dc in range(2) if (dy, dz) != (0, 0)]
+    peers = [(at(dc=1), st)] + [(at(dy, dz, dc), st) for dy in range(4) for dz in range(2) for dc in range(2) if (dy != 0) != (dz != 0)]
     peers += [(tm, sat(dx, dl)) for dx in range(4) for dl in range(2) if (dx, dl) != (0, 0)]
     for peer in peers:
         pl.semaphore_signal(barrier, inc=1, device_id=peer, device_id_type=MESH)
-    pl.semaphore_wait(barrier, len(peers))
 
     sends = []
 
@@ -87,9 +89,6 @@
     def arrive(dst, rsem):
         pltpu.make_async_remote_copy(dst, dst, ssem.at[0], rsem, device_id=(tm, st), device_id_type=MESH).wait_recv()
 
-    load_fw.wait()
-    send(fw.at[pl.ds(rows - 16, 16), :], tail, tailsem.at[0], (nxt, st))
-    load_lr.wait()
 
     def drive(s):
         loads[s].wait()
@@ -97,9 +96,11 @@
         parts = part.reshape(2, rows, 512)
         acc[s] = jnp.where(c == 0, parts[0], parts[1])
         cs[s] = jnp.where(c == 0, parts[1], parts[0])
-        send(cs.at[s], cr.at[s], csem.at[s], (at(dc=1), st))
         if s + spk.shape[0] < 8:
             loads[s + spk.shape[0]] = spike_load(s + spk.shape[0])
+
+    def swap(s):
+        send(cs.at[s], cr.at[s], csem.at[s], (at(dc=1), st))
 
     def pair_up(s):
         dy, dz = STEPS[s]
@@ -144,26 +145,30 @@
             value = value + decode(p1r[i], p1rc[i])
         return value
 
-    drive(0)
-    arrive(tail, tailsem.at[0])
-    turned = pltpu.roll(fw[...].astype(F32), 1, 0)
-    above = jnp.broadcast_to(tail[...].astype(F32)[15:16, :], (rows, 512))
-    at_top = lax.broadcasted_iota(jnp.int32, (rows, 512), 0) == 0
-    fg[st] = jnp.where(at_top, above, turned).astype(BF16)
+    load_lr.wait()
+    for s in range(EARLY):
+        drive(s)
+    load_fw.wait()
+    fg[st] = fw[...]
+    pl.semaphore_wait(barrier, len(peers))
+    swap(0)
     send(fg.at[st], fg.at[st], f1sem.at[st], (tm, sat(0, 1)))
     for dx in (1, 3, 2):
         send(fg.at[st], fg.at[st], f1sem.at[st], (tm, sat(dx)))
-    for s in range(1, 8):
-        drive(s)
-        pair_up(s - 1)
-        if s == 2:
-            other = sat(0, 1)
+    for s in range(1, EARLY):
+        swap(s)
+    other = sat(0, 1)
+    for s in range(8):
+        pair_up(s)
+        if s + EARLY < 8:
+            drive(s + EARLY)
+            swap(s + EARLY)
+        if s == RELAY:
             arrive(fg.at[other], f1sem.at[other])
             for dx in (1, 3, 2):
                 send(fg.at[other], fg.at[other], f1sem.at[other], (tm, sat(dx)))
         if s >= 6:
             q_second(s - 2)
-    pair_up(7)
     q_second(6)
     value = p_sum(3)
     p2s[0], p2sc[0] = encode(value)
@@ -173,6 +178,7 @@
     q_second(7)
 
     load_tr.wait()
+    load_mask.wait()
 
     @pl.loop(0, STATES // BLOCK)
     def _(ib):
@@ -183,34 +189,27 @@
             at_cols = pl.ds(cb * BLOCK, BLOCK)
             am[at_rows, at_cols] = (tr[at_rows, at_cols].astype(F32) * keep).astype(BF16)
 
-    for dl in (0, 1):
-        for dx in (1, 3, 2):
-            who = sat(dx, dl)
-            arrive(fg.at[who], f1sem.at[who])
     owner = x // 2
     quarter = x % 2
     mine = c == owner
     qcols = pl.ds(pl.multiple_of(x * 128, 128), 128)
-    f2 = []
-    for dy, dz in STEPS:
+    handed = []
+    for n, (dx, dl) in enumerate(((0, 0), (0, 1), (1, 0), (3, 0), (2, 0), (1, 1), (3, 1), (2, 1))):
+        who = sat(dx, dl)
+        if n > 1:
+            arrive(fg.at[who], f1sem.at[who])
+        src = fg.at[who, :, qcols]
+        dst = fr.at[quarter, tm]
+        to = who * 2 + owner
         i = len(sends)
-        to_group = ((y + dy) % 4) * 2 + (zh + dz) % 2
-        src = fg.at[to_group, :, qcols]
-        dst = fr.at[quarter, tm]
-        cp = pltpu.make_async_remote_copy(src, dst, ssem.at[i], f2sem.at[tm], device_id=(to_group * 2 + owner, st), device_id_type=MESH)
-        sends.append(cp)
-        if (dy, dz) != (0, 0):
-            cp.start()
-        else:
-            own_cp = pltpu.make_async_copy(src, dst, f2sem.at[tm])
-            pl.when(mine)(own_cp.start)
-            pl.when(jnp.logical_not(mine))(cp.start)
-            sends.pop()
-            last_f2 = cp
-            sends.append(None)
-    car[...] = jnp.zeros_like(car)
-    for b in range(8):
-        car[...] += jnp.dot(fg[b], am[pl.ds(b * 512, 512), :], preferred_element_type=F32)
+        sends.append(None)
+        cp = pltpu.make_async_remote_copy(src, dst, ssem.at[i], f2sem.at[tm], device_id=(to, st), device_id_type=MESH)
+        pl.when(to == tm)(pltpu.make_async_copy(src, dst, f2sem.at[tm]).start)
+        pl.when(to != tm)(cp.start)
+        handed.append((to, cp))
+        part = jnp.dot(fg[who], am[pl.ds(pl.multiple_of(who * 512, 512), 512), :], preferred_element_type=F32)
+        car[...] = part if n == 0 else car[...] + part
+    send(car.at[pl.ds(rows - 8, 8), :], tail, tailsem.at[0], (nxt, st))
 
     load_bw.wait()
     load_rt.wait()
@@ -225,6 +224,8 @@
         arrive(q2r.at[i], q2sem.at[0, i])
         arrive(q2rc.at[i], q2sem.at[1, i])
         q_drive = q_drive + decode(q2r[i], q2rc[i])
+    arrive(tail, tailsem.at[0])
+    at_top = lax.broadcasted_iota(jnp.int32, (rows, half), 0) == 0
     is_edge = jnp.logical_and(lax.broadcasted_iota(jnp.int32, (rows, half), 0) == 0, tm == 0)
     ahead = []
     total = jnp.zeros((rows, 1), F32)
@@ -233,7 +234,8 @@
         term = jnp.exp(drive_sum - rt[:, cols]) * bw[:, cols]
         term = jnp.where(is_edge, jnp.broadcast_to(ew[:, cols], (rows, half)), term)
         acc[0, :, cols] = term
-        total = total + jnp.sum(term * car[:, cols], axis=1, keepdims=True)
+        carried = jnp.where(at_top, jnp.broadcast_to(tail[7:8, cols], (rows, half)), pltpu.roll(car[:, cols], 1, 0))
+        total = total + jnp.sum(term * carried, axis=1, keepdims=True)
     tcol[pl.ds(0, rows), :] = jnp.broadcast_to(total, (rows, 128))
     tcol[pl.ds(rows, 256 - rows), :] = jnp.ones((256 - rows, 128), F32)
     tot[st] = tcol[...].T[0:8, :]
@@ -314,25 +316,22 @@
         @pl.when(jnp.logical_not(jnp.logical_and(mine, quarter == q)))
         def _(q=q):
             pltpu.make_async_remote_copy(fr.at[q], fr.at[q], f3sem.at[0, 0], f3sem.at[1, q], device_id=(tm, st), device_id_type=MESH).wait_recv()
-    for dy, dz in STEPS:
-        for h in (0, 1):
-            w_arrive(h, at(dy, dz, 1), 1)
-
+        lt[pl.ds(q * 128, 128), :] = pltpu.roll(fr[q].reshape(16 * rows, 128).astype(F32), 1, 0).T.astype(BF16)
+    at_rows = pl.ds(pl.multiple_of(tm * 256, 256), 256)
     scale = STATES * STATES / time_total
     for h in range(2):
-        right = w[h].reshape(16 * rows, half)
-        for q in range(2):
-            left = fr[q].reshape(16 * rows, 128)
-            pair = lax.dot_general(left, right, (((0,), (0,)), ((), ())), preferred_element_type=F32)
-            at_rows = pl.ds(pl.multiple_of(tm * 256 + q * 128, 128), 128)
-            moves = am[at_rows, pl.ds(h * half, half)].astype(F32)
-            out[pl.ds(q * 128, 128), pl.ds(h * half, half)] = moves * pair * scale
-    store = local(out, counts, 10)
+        for dy, dz in STEPS:
+            w_arrive(h, at(dy, dz, 1), 1)
+        pair = jnp.dot(lt[...], w[h].reshape(16 * rows, half), preferred_element_type=F32)
+        at_cols = pl.ds(h * half, half)
+        out[:, at_cols] = am[at_rows, at_cols].astype(F32) * pair * scale
+    store = local(out, counts, 14)
 
     for i, cp in enumerate(sends):
         if cp is not None:
             cp.wait_send()
-    pl.when(jnp.logical_not(mine))(last_f2.wait_send)
+    for to, cp in handed:
+        pl.when(to != tm)(cp.wait_send)
 
     @pl.when(mine)
     def _():
@@ -340,6 +339,11 @@
             pltpu.make_async_remote_copy(fr.at[quarter], fr.at[quarter], f3sem.at[0, dx], f3sem.at[1, quarter],
                                          device_id=(tm, sat(dx)), device_id_type=MESH).wait_send()
     store.wait()
+
+
+def place(counts, loglik, counts_out, loglik_out):
+    counts_out[...] = counts[...]
+    loglik_out[...] = loglik[0, 0:loglik_out.shape[0]]
 
 
 def shards(spikes, log_rate, forward, backward, transition, rate_total, edge_weight, block_mask):
@@ -349,28 +353,31 @@
     vm = pltpu.VMEM
     dma = pltpu.SemaphoreType.DMA
     scratch = [
-        vm((3, 2 * rows, neurons), jnp.int32), vm((neurons, width), BF16), vm((rows, width), BF16), vm((rows, width), F32),
+        pltpu.SMEM(block_mask.shape, jnp.int32), vm((256, 16 * rows), BF16), vm((8, 2 * rows, neurons), jnp.int32), vm((neurons, width), BF16), vm((rows, width), BF16), vm((rows, width), F32),
         vm((STATES, width), BF16), vm((STATES, width), BF16), vm((1, width), F32), vm((1, width), F32), vm((256, width), F32),
-        vm((16, width), BF16), vm((8, rows, width), BF16), vm((2, 16, rows, 128), BF16),
+        vm((8, width), F32), vm((8, rows, width), BF16), vm((2, 16, rows, 128), BF16),
         vm((8, rows, width), F32), vm((8, rows, width), F32), vm((8, rows, width), F32),
     ]
     for n in (6, 4, 3, 1):
         scratch += [vm((n, rows, 256), I16), vm((n, rows, 256), I16), vm((n, 8, 256), F32), vm((n, 8, 256), F32)]
     scratch += [
         vm((rows, width), F32), vm((256, 128), F32), vm((8, 8, 256), F32), vm((8, 256), F32), vm((8, 256), F32), vm((2, 16, rows, 256), BF16),
-        dma((11,)), dma((120,)), dma((8,)), dma((1,)), dma((8,)), dma((16,)), dma((2, 4)), dma((2, 6)), dma((2, 4)), dma((2, 3)), dma((2,)),
+        dma((20,)), dma((120,)), dma((8,)), dma((1,)), dma((8,)), dma((16,)), dma((2, 4)), dma((2, 6)), dma((2, 4)), dma((2, 3)), dma((2,)),
         dma((8,)), dma((1,)), dma((2, 16)), dma((2, 16)),
     ]
     hbm = pl.BlockSpec(memory_space=pl.ANY)
     counts, loglik = pl.pallas_call(
         functools.partial(kernel, time_total),
         out_shape=(jax.ShapeDtypeStruct((256, width), F32), jax.ShapeDtypeStruct((8, 256), F32)),
-        in_specs=[hbm] * 7 + [pl.BlockSpec(memory_space=pltpu.SMEM)],
+        in_specs=[hbm] * 8,
         out_specs=(hbm, pl.BlockSpec(memory_space=pltpu.VMEM)),
         scratch_shapes=scratch,
         compiler_params=pltpu.CompilerParams(collective_id=0, has_side_effects=True, vmem_limit_bytes=56 * 2**20),
     )(spikes, log_rate, forward, backward, transition, rate_total.reshape(1, width), edge_weight.reshape(1, width), block_mask)
-    return counts, loglik[0, :rows]
+    return pl.pallas_call(
+        place,
+        out_shape=(jax.ShapeDtypeStruct((256, width), F32), jax.ShapeDtypeStruct((rows,), F32)),
+    )(counts, loglik)
 
 
 def solution(mesh):

time: 57.8 us -> 54.2 us (0.938)
  local copies, waits for them, and re-layouts: 3.13 us -> 0 us
    pallas_call x1, Pallas kernels: 53.8 us -> 51.6 us  [shards(): pl.pallas_call(functools.partial(kernel, time_total), out_shape=(jax.Shap...]
    pallas_call x0 -> x1, Pallas kernels: none -> 1.87 us  [shards(): pl.pallas_call(place, out_shape=(jax.ShapeDtypeStruct((256, width), F32),...]
    unnamed x1 -> x0, local copies, waits for them, and re-layouts: 1.87 us -> none
    slice x1 -> x0, local copies, waits for them, and re-layouts: 1.26 us -> none  [shards(): return (counts, loglik[0, :rows])]
where the time goes in v2:
time: 54.2 us; the launch traced here: 54.1 us
  Pallas kernels  53.4 us (99%)
  between operations  0.64 us (1%)
    pallas_call x1, Pallas kernels, shards(): pl.pallas_call(functools.partial(kernel, time_total), out_shape=(jax.Shap...  51.6 us
    pallas_call x1, Pallas kernels, shards(): pl.pallas_call(place, out_shape=(jax.ShapeDtypeStruct((256, width), F32),...  1.87 us

profile of v2, /device:TPU:1, one launch (start us, length us, event | category | flops | bytes accessed | tf_op | source)
XLA Modules:
  0.0 54.1 jit_solution(17027883809821042152)
XLA Ops:
  0.6 51.6 %shard_map.95 = (f32[256,512]{1,0:T(8,128)}, f32[8,256]{1,0:T(8,128)}) custom-call(s32[2304,2048]{1,0:T(8,128)} %spikes.1, bf16[2048,512]{1,0:T(8,128)(2,1)} %log_rate.1, bf16[144,512]{1,0:T(8,128)(2,1)} %forward.1, f32[144,512]{1,0:T(8,128)} %backward.1, bf16[4096,512]{1,0:T(8,128)(2,1)} %transition.1, f32[1,512]{1,0:T(1,128)} %bitcast.2, ...), custom_call_target="tpu_custom_call" | custom-call | tf_op jit(solution)/shard_map/pallas_call | solution.py:369
  52.2 1.9 %shard_map.96 = (f32[256,512]{1,0:T(8,128)}, f32[144]{0:T(256)}) custom-call(f32[256,512]{1,0:T(8,128)} %get-tuple-element.4.counts, f32[8,256]{1,0:T(8,128)} %get-tuple-element.5.loglik), custom_call_target="tpu_custom_call" | custom-call | tf_op jit(solution)/shard_map/pallas_call | solution.py:377

commit v3 on v2

v3 whole, which is shorter than its diff:
```python
import functools
import jax
import jax.numpy as jnp
from jax import lax
from jax.experimental import pallas as pl
from jax.experimental.pallas import tpu as pltpu
from jax.sharding import PartitionSpec as P

MESH = pl.DeviceIdType.MESH
STATES = 4096
BLOCK = 128
F32, BF16, I16 = jnp.float32, jnp.bfloat16, jnp.int16
TOP = 32760.0
ROUND = 12582912.0
STEPS = ((2, 1), (1, 1), (3, 1), (0, 1), (2, 0), (1, 0), (3, 0), (0, 0))
YS = (2, 1, 3)
EARLY = 3
RELAY = 4


def encode(value):
    most = jnp.maximum(jnp.max(jnp.abs(value), axis=0, keepdims=True), 1e-30)
    coded = (value * (TOP / most) + ROUND) - ROUND
    return coded.astype(jnp.int32).astype(I16), jnp.broadcast_to(most * (1.0 / TOP), (8, value.shape[1]))


def decode(coded, scale):
    return coded.astype(jnp.int32).astype(F32) * scale[0:1, :]


def kernel(time_total, spikes, log_rate, forward, backward, transition, rate, edge, block_mask,
           counts, loglik,
           mask, lt, spk, lr, fw, bw, tr, am, rt, ew,
           fg, fr, cs, cr, acc,
           p1s, p1r, p1sc, p1rc, q1s, q1r, q1sc, q1rc, q2s, q2r, q2sc, q2rc, p2s, p2r, p2sc, p2rc,
           car, tcol, tot, tsum, first, w,
           lsem, ssem, csem, tailsem, f1sem, f1tsem, handsem, f2sem, f3sem, p1sem, q1sem, q2sem, p2sem, totsem, firstsem, wsem, coresem):
    tm, st = lax.axis_index("tm"), lax.axis_index("state")
    y, zh, c = tm // 4, (tm // 2) % 2, tm % 2
    zl, x = st // 4, st % 4

    def at(dy=0, dz=0, dc=0):
        return (((y + dy) % 4) * 2 + (zh + dz) % 2) * 2 + (c + dc) % 2

    def sat(dx=0, dl=0):
        return ((zl + dl) % 2) * 4 + (x + dx) % 4

    rows = fw.shape[0]
    group = 2 * rows
    half = 256

    def local(src, dst, i):
        cp = pltpu.make_async_copy(src, dst, lsem.at[i])
        cp.start()
        return cp

    def spike_load(s):
        dy, dz = STEPS[s]
        row = pl.multiple_of((((y + dy) % 4) * 2 + (zh + dz) % 2) * group, group)
        return local(spikes.at[pl.ds(row, group), :], spk.at[s % spk.shape[0]], s % spk.shape[0])

    loads = {}
    load_fw = local(forward, fw, 8)
    load_lr = local(log_rate, lr, 9)
    for s in range(spk.shape[0]):
        loads[s] = spike_load(s)
    load_tr = local(transition, tr, 10)
    load_mask = local(block_mask, mask, 15)
    load_bw = local(backward, bw, 11)
    load_rt = local(rate, rt, 12)
    load_ew = local(edge, ew, 13)

    barrier = pltpu.get_barrier_semaphore()
    prev, nxt = (tm + 15) % 16, (tm + 1) % 16
    peers = [(at(dc=1), st)] + [(at(dy, dz, dc), st) for dy in range(4) for dz in range(2) for dc in range(2) if (dy != 0) != (dz != 0)]
    peers += [(tm, sat(dx, dl)) for dx in range(4) for dl in range(2) if (dx, dl) != (0, 0)]
    peers += [(prev, st), (nxt, st)]
    for peer in peers:
        pl.semaphore_signal(barrier, inc=1, device_id=peer, device_id_type=MESH)

    def send(src, dst, i, rsem, device):
        pltpu.make_async_remote_copy(src, dst, ssem.at[i], rsem, device_id=device, device_id_type=MESH).start()

    def sent(ref, i):
        pltpu.make_async_remote_copy(ref, ref, ssem.at[i], ssem.at[i], device_id=(tm, st), device_id_type=MESH).wait_send()

    def arrive(dst, rsem):
        pltpu.make_async_remote_copy(dst, dst, ssem.at[0], rsem, device_id=(tm, st), device_id_type=MESH).wait_recv()


    def drive(s):
        loads[s].wait()
        part = jnp.dot(spk[s % spk.shape[0]].astype(F32).astype(BF16), lr[...], preferred_element_type=F32)
        parts = part.reshape(2, rows, 512)
        acc[s] = jnp.where(c == 0, parts[0], parts[1])
        cs[s] = jnp.where(c == 0, parts[1], parts[0])
        if s + spk.shape[0] < 8:
            loads[s + spk.shape[0]] = spike_load(s + spk.shape[0])

    def swap(s):
        send(cs.at[s], cr.at[s], 0, csem.at[s], (at(dc=1), st))

    def pair_up(s):
        dy, dz = STEPS[s]
        arrive(cr.at[s], csem.at[s])
        if dy != 0:
            i = dz * 3 + dy - 1
            p1s[i], p1sc[i] = encode(acc[s, :, 0:half] + cr[s, :, 0:half])
            to = (at(dy), st)
            send(p1s.at[i], p1r.at[i], 4, p1sem.at[0, i], to)
            send(p1sc.at[i], p1rc.at[i], 5, p1sem.at[1, i], to)
        else:
            acc[s, :, 0:half] += cr[s, :, 0:half]
        if dz != 0:
            q1s[dy], q1sc[dy] = encode(acc[s, :, half:] + cr[s, :, half:])
            to = (at(0, 1), st)
            send(q1s.at[dy], q1r.at[dy], 6, q1sem.at[0, dy], to)
            send(q1sc.at[dy], q1rc.at[dy], 7, q1sem.at[1, dy], to)
        else:
            acc[s, :, half:] += cr[s, :, half:]

    def q_second(s):
        dy, _ = STEPS[s]
        arrive(q1r.at[dy], q1sem.at[0, dy])
        arrive(q1rc.at[dy], q1sem.at[1, dy])
        value = acc[s, :, half:] + decode(q1r[dy], q1rc[dy])
        if dy == 0:
            acc[s, :, half:] = value
        else:
            i = dy - 1
            q2s[i], q2sc[i] = encode(value)
            to = (at(dy), st)
            send(q2s.at[i], q2r.at[i], 8, q2sem.at[0, i], to)
            send(q2sc.at[i], q2rc.at[i], 9, q2sem.at[1, i], to)

    def p_sum(s):
        dz = STEPS[s][1]
        value = acc[s, :, 0:half]
        for dy in YS:
            i = dz * 3 + dy - 1
            arrive(p1r.at[i], p1sem.at[0, i])
            arrive(p1rc.at[i], p1sem.at[1, i])
            value = value + decode(p1r[i], p1rc[i])
        return value

    own = pl.ds(16, rows)
    head = pl.ds(0, 16)

    def spread(who, dx, dl):
        send(fg.at[who, own], fg.at[who, own], 1, f1sem.at[who], (tm, sat(dx, dl)))

    load_fw.wait()
    fg[st, 16:16 + rows, :] = fw[...]
    load_lr.wait()
    drive(0)
    pl.semaphore_wait(barrier, len(peers))
    swap(0)
    send(fg.at[st, pl.ds(rows, 16)], fg.at[st, head], 3, tailsem.at[0], (nxt, st))
    spread(st, 0, 1)
    for dx in (1, 3, 2):
        spread(st, dx, 0)
    other = sat(0, 1)
    for s in range(8):
        if s < 7:
            drive(s + 1)
            swap(s + 1)
        pair_up(s)
        if s == 3:
            arrive(fg.at[st, head], tailsem.at[0])
            for dx in range(4):
                for dl in range(2):
                    if (dx, dl) != (0, 0):
                        send(fg.at[st, head], fg.at[st, head], 2, f1tsem.at[0], (tm, sat(dx, dl)))
        if s == RELAY:
            arrive(fg.at[other, own], f1sem.at[other])
            for dx in (1, 3, 2):
                spread(other, dx, 0)

    load_tr.wait()
    load_mask.wait()

    @pl.loop(0, STATES // BLOCK)
    def _(ib):
        for cb in range(4):
            jb = st * 4 + cb
            keep = jnp.maximum(mask[ib, jb], (ib == jb).astype(jnp.int32)).astype(F32)
            at_rows = pl.ds(pl.multiple_of(ib * BLOCK, BLOCK), BLOCK)
            at_cols = pl.ds(cb * BLOCK, BLOCK)
            am[at_rows, at_cols] = (tr[at_rows, at_cols].astype(F32) * keep).astype(BF16)

    q_second(4)
    q_second(5)
    q_second(6)
    value = p_sum(3)
    p2s[0], p2sc[0] = encode(value)
    to = (at(0, 1), st)
    send(p2s.at[0], p2r.at[0], 10, p2sem.at[0], to)
    send(p2sc.at[0], p2rc.at[0], 11, p2sem.at[1], to)
    q_second(7)

    owner = x // 2
    quarter = x % 2
    mine = c == owner
    qcols = pl.ds(pl.multiple_of(x * 128, 128), 128)
    handed = []
    arrive(fg.at[pl.ds(0, 7), head], f1tsem.at[0])
    for n, (dx, dl) in enumerate(((0, 0), (0, 1), (1, 0), (3, 0), (2, 0), (1, 1), (3, 1), (2, 1))):
        who = sat(dx, dl)
        if n > 1:
            arrive(fg.at[who, own], f1sem.at[who])
        src = fg.at[who, own, qcols]
        dst = fr.at[quarter, tm]
        to = who * 2 + owner
        cp = pltpu.make_async_remote_copy(src, dst, handsem.at[n], f2sem.at[0], device_id=(to, st), device_id_type=MESH)
        pl.when(to == tm)(pltpu.make_async_copy(src, dst, f2sem.at[1]).start)
        pl.when(to != tm)(cp.start)
        handed.append((to, cp))
        part = jnp.dot(fg[who], am[pl.ds(pl.multiple_of(who * 512, 512), 512), :], preferred_element_type=F32)
        car[...] = part if n == 0 else car[...] + part
    load_bw.wait()
    load_rt.wait()
    load_ew.wait()
    value = p_sum(7)
    arrive(p2r.at[0], p2sem.at[0])
    arrive(p2rc.at[0], p2sem.at[1])
    p_drive = value + decode(p2r[0], p2rc[0])
    q_drive = acc[7, :, half:]
    for dy in YS:
        i = dy - 1
        arrive(q2r.at[i], q2sem.at[0, i])
        arrive(q2rc.at[i], q2sem.at[1, i])
        q_drive = q_drive + decode(q2r[i], q2rc[i])
    moved = pltpu.roll(car[...], 1, 0)
    is_edge = jnp.logical_and(lax.broadcasted_iota(jnp.int32, (rows, half), 0) == 0, tm == 0)
    ahead = []
    total = jnp.zeros((rows, 1), F32)
    for h, drive_sum in enumerate((p_drive, q_drive)):
        cols = slice(h * half, (h + 1) * half)
        term = jnp.exp(drive_sum - rt[:, cols]) * bw[:, cols]
        term = jnp.where(is_edge, jnp.broadcast_to(ew[:, cols], (rows, half)), term)
        acc[0, :, cols] = term
        carried = moved[16:, cols]
        total = total + jnp.sum(term * carried, axis=1, keepdims=True)
    tcol[pl.ds(0, rows), :] = jnp.broadcast_to(total, (rows, 128))
    tcol[pl.ds(rows, 256 - rows), :] = jnp.ones((256 - rows, 128), F32)
    tot[st] = tcol[...].T[0:8, :]
    for dx, dl in ((2, 1), (2, 0), (1, 1), (3, 1), (1, 0), (3, 0), (0, 1)):
        send(tot.at[st], tot.at[st], 12, totsem.at[0], (tm, sat(dx, dl)))

    def hand_on(q, n, dx, i):
        part = fr.at[q, pl.ds(8 * n, 8)]
        return pltpu.make_async_remote_copy(part, part, ssem.at[i], f3sem.at[2 * q + n], device_id=(tm, sat(dx)), device_id_type=MESH)

    def handed_part(q, n):
        arrive(fr.at[q, pl.ds(8 * n, 8)], f3sem.at[2 * q + n])

    @pl.when(mine)
    def _():
        pltpu.make_async_copy(fr.at[quarter, tm], fr.at[quarter, tm], f2sem.at[1]).wait()
        arrive(fr.at[quarter, pl.ds(0, 15)], f2sem.at[0])
        hand_on(quarter, 0, 1, 16).start()
        hand_on(quarter, 1, 3, 17).start()
        hand_on(quarter, 1, 1, 18).start()
        hand_on(quarter, 0, 3, 19).start()

    arrive(tot.at[pl.ds(0, 7)], totsem.at[0])
    sums = tot[0]
    for b in range(1, 8):
        sums = sums + tot[b]
    tsum[...] = sums
    tcol[...] = jnp.broadcast_to(sums[0:1, :], (128, 256)).T
    norm = tcol[pl.ds(0, rows), :]
    for h in range(2):
        for q in range(2):
            cols = pl.ds(h * half + q * 128, 128)
            w[h, c, tm // 2, :, pl.ds(q * 128, 128)] = (acc[0, :, cols] / norm).astype(BF16)

    def w_send(h, who, dy, dz, dc=0):
        send(w.at[h, c, who // 2], w.at[h, c, who // 2], 14 + h, coresem.at[h] if dc else wsem.at[h, who // 2], (at(dy, dz, dc), st))

    def w_arrive(h, who):
        arrive(w.at[h, c, who // 2], wsem.at[h, who // 2])

    w_send(0, tm, 0, 1)
    for dy in YS:
        w_send(1, tm, dy, 0)
    for dy in YS:
        w_send(0, tm, dy, 0)
    w_send(1, tm, 0, 1)
    w_send(0, tm, 0, 0, 1)
    w_send(1, tm, 0, 0, 1)
    send(tsum, first, 13, firstsem.at[0], (prev, st))

    opp = at(0, 1)
    w_arrive(0, opp)
    for dy in YS:
        w_send(0, opp, dy, 0)
    w_send(0, opp, 0, 0, 1)
    for dy in (1, 3, 2):
        who = at(dy, 0)
        w_arrive(1, who)
        w_send(1, who, 0, 1)
        w_send(1, who, 0, 0, 1)
    for q in range(2):
        away = (x + 4 - 2 * c - q) % 4

        @pl.when(away == 1)
        def _(q=q):
            handed_part(q, 0)
            hand_on(q, 0, 1, 20).start()

        @pl.when(away == 3)
        def _(q=q):
            handed_part(q, 1)
            hand_on(q, 1, 3, 20).start()

    for dy in (1, 3, 2):
        who = at(dy, 0)
        w_arrive(0, who)
        w_send(0, who, 0, 0, 1)
    w_arrive(1, opp)
    w_send(1, opp, 0, 0, 1)
    for dy in (1, 3):
        for h in (0, 1):
            who = at(dy, 1)
            w_arrive(h, who)
            w_send(h, who, 0, 0, 1)
    arrive(first, firstsem.at[0])
    lanes = lax.broadcasted_iota(jnp.int32, (8, 256), 1)
    here = pltpu.roll(tsum[...], 255, 1)
    there = jnp.broadcast_to(first[...][:, 0:1], (8, 256))
    loglik[...] = jnp.log(jnp.where(lanes == rows - 1, there, here))
    for h in (0, 1):
        who = at(2, 1)
        w_arrive(h, who)
        w_send(h, who, 0, 0, 1)
    for q in range(2):
        away = (x + 4 - 2 * c - q) % 4
        pl.when(jnp.logical_or(away == 2, away == 3))(functools.partial(handed_part, q, 0))
        pl.when(jnp.logical_or(away == 2, away == 1))(functools.partial(handed_part, q, 1))
        later = pltpu.roll(fr[q].reshape(16 * rows, 128).astype(F32), 1, 0).reshape(8, 2, rows, 128)
        for k in range(2):
            lt[k, pl.ds(q * 128, 128), :] = later[:, k].reshape(8 * rows, 128).T.astype(BF16)
    at_rows = pl.ds(pl.multiple_of(tm * 256, 256), 256)
    scale = STATES * STATES / time_total
    pair = [jnp.dot(lt[c], w[h, c].reshape(8 * rows, half), preferred_element_type=F32) for h in range(2)]
    for h in range(2):
        arrive(w.at[h, 1 - c], coresem.at[h])
        both = pair[h] + jnp.dot(lt[1 - c], w[h, 1 - c].reshape(8 * rows, half), preferred_element_type=F32)
        at_cols = pl.ds(h * half, half)
        counts[:, at_cols] = am[at_rows, at_cols].astype(F32) * both * scale

    sent(cs, 0)
    sent(fg.at[pl.ds(0, 7), own], 1)
    sent(fg.at[pl.ds(0, 7), head], 2)
    sent(fg.at[0, head], 3)
    for i, ref in enumerate((p1s, p1sc, q1s, q1sc, q2s, q2sc, p2s, p2sc)):
        sent(ref, 4 + i)
    sent(tot.at[pl.ds(0, 7)], 12)
    sent(tsum, 13)
    for h in range(2):
        sent(w.at[h, 0], 14 + h)
        sent(w.at[h, 1, pl.ds(0, 7)], 14 + h)
    for to, cp in handed:
        pl.when(to != tm)(cp.wait_send)

    @pl.when(mine)
    def _():
        for n, (m, dx) in enumerate(((0, 1), (1, 3), (1, 1), (0, 3))):
            hand_on(quarter, m, dx, 16 + n).wait_send()

    sent(fr.at[0, pl.ds(0, 8)], 20)


def place(counts, loglik, counts_out, loglik_out):
    counts_out[...] = counts[...]
    loglik_out[...] = loglik[0, 0:loglik_out.shape[0]]


def shards(spikes, log_rate, forward, backward, transition, rate_total, edge_weight, block_mask):
    rows = forward.shape[0]
    time_total = spikes.shape[0]
    neurons, width = log_rate.shape
    vm = pltpu.VMEM
    dma = pltpu.SemaphoreType.DMA
    scratch = [
        pltpu.SMEM(block_mask.shape, jnp.int32), vm((2, 256, 8 * rows), BF16), vm((8, 2 * rows, neurons), jnp.int32), vm((neurons, width), BF16), vm((rows, width), BF16), vm((rows, width), F32),
        vm((STATES, width), BF16), vm((STATES, width), BF16), vm((1, width), F32), vm((1, width), F32),
        vm((8, 16 + rows, width), BF16), vm((2, 16, rows, 128), BF16),
        vm((8, rows, width), F32), vm((8, rows, width), F32), vm((8, rows, width), F32),
    ]
    for n in (6, 4, 3, 1):
        scratch += [vm((n, rows, 256), I16), vm((n, rows, 256), I16), vm((n, 8, 256), F32), vm((n, 8, 256), F32)]
    scratch += [
        vm((16 + rows, width), F32), vm((256, 128), F32), vm((8, 8, 256), F32), vm((8, 256), F32), vm((8, 256), F32), vm((2, 2, 8, rows, 256), BF16),
        dma((16,)), dma((21,)), dma((8,)), dma((1,)), dma((8,)), dma((1,)), dma((8,)), dma((2,)), dma((4,)),
        dma((2, 6)), dma((2, 4)), dma((2, 3)), dma((2,)), dma((1,)), dma((1,)), dma((2, 8)), dma((2,)),
    ]
    hbm = pl.BlockSpec(memory_space=pl.ANY)
    counts, loglik = pl.pallas_call(
        functools.partial(kernel, time_total),
        out_shape=(vm((256, width), F32), vm((8, 256), F32)),
        in_specs=[hbm] * 8,
        out_specs=(pl.BlockSpec(memory_space=pltpu.VMEM), pl.BlockSpec(memory_space=pltpu.VMEM)),
        scratch_shapes=scratch,
        compiler_params=pltpu.CompilerParams(collective_id=0, has_side_effects=True, vmem_limit_bytes=56 * 2**20),
    )(spikes, log_rate, forward, backward, transition, rate_total.reshape(1, width), edge_weight.reshape(1, width), block_mask)
    return pl.pallas_call(
        place,
        out_shape=(jax.ShapeDtypeStruct((256, width), F32), jax.ShapeDtypeStruct((rows,), F32)),
    )(pltpu.with_memory_space_constraint(counts, pltpu.VMEM), pltpu.with_memory_space_constraint(loglik, pltpu.VMEM))


def solution(mesh):
    in_specs = (P(None, "tm"), P("tm", "state"), P("tm", "state"), P("tm", "state"), P(None, "state"), P("state"), P("state"), P())
    out_specs = (P("tm", "state"), P("tm"))
    return jax.shard_map(shards, mesh=mesh, in_specs=in_specs, out_specs=out_specs, check_vma=False)
```

time: 54.2 us -> 48.9 us (0.902)
  Pallas kernels: 53.4 us -> 48.2 us
    pallas_call x1, Pallas kernels: 51.6 us -> 47.3 us  [shards(): pl.pallas_call(functools.partial(kernel, time_total), out_shape=(vm((256,...]
    pallas_call x1, Pallas kernels: 1.87 us -> 0.83 us  [shards(): pl.pallas_call(place, out_shape=(jax.ShapeDtypeStruct((256, width), F32),...]
where the time goes in v3:
time: 48.9 us; the launch traced here: 48.8 us
  Pallas kernels  48.2 us (99%)
  between operations  0.64 us (1%)
    pallas_call x1, Pallas kernels, shards(): pl.pallas_call(functools.partial(kernel, time_total), out_shape=(vm((256,...  47.3 us

profile of v3, /device:TPU:1, one launch (start us, length us, event | category | flops | bytes accessed | tf_op | source)
XLA Modules:
  0.0 48.8 jit_solution(10572343890717987052)
XLA Ops:
  0.6 47.3 %shard_map.95 = (f32[256,512]{1,0:T(8,128)S(1)}, f32[8,256]{1,0:T(8,128)S(1)}) custom-call(s32[2304,2048]{1,0:T(8,128)} %spikes.1, bf16[2048,512]{1,0:T(8,128)(2,1)} %log_rate.1, bf16[144,512]{1,0:T(8,128)(2,1)} %forward.1, f32[144,512]{1,0:T(8,128)} %backward.1, bf16[4096,512]{1,0:T(8,128)(2,1)} %transition.1, f32[1,512]{1,0:T(1,128)} %bitcast.2, ...), custom_call_target="tpu_custom_call" | custom-call | tf_op jit(solution)/shard_map/pallas_call | solution.py:400
  48.0 0.8 %shard_map.96 = (f32[256,512]{1,0:T(8,128)}, f32[144]{0:T(256)}) custom-call(f32[256,512]{1,0:T(8,128)S(1)} %get-tuple-element.4.counts, f32[8,256]{1,0:T(8,128)S(1)} %get-tuple-element.5.loglik), custom_call_target="tpu_custom_call" | custom-call | tf_op jit(solution)/shard_map/pallas_call | solution.py:408

commit v4 on v3

--- a/solution.py
+++ b/solution.py
@@ -15,7 +15,7 @@
 STEPS = ((2, 1), (1, 1), (3, 1), (0, 1), (2, 0), (1, 0), (3, 0), (0, 0))
 YS = (2, 1, 3)
 EARLY = 3
-RELAY = 4
+RELAY = 3
 
 
 def encode(value):
@@ -30,7 +30,7 @@
 
 def kernel(time_total, spikes, log_rate, forward, backward, transition, rate, edge, block_mask,
            counts, loglik,
-           mask, lt, spk, lr, fw, bw, tr, am, rt, ew,
+           mask, lt, spk, lr, fw, bw, tr, am, rt, ew, pair,
            fg, fr, cs, cr, acc,
            p1s, p1r, p1sc, p1rc, q1s, q1r, q1sc, q1rc, q2s, q2r, q2sc, q2rc, p2s, p2r, p2sc, p2rc,
            car, tcol, tot, tsum, first, w,
@@ -176,6 +176,12 @@
             for dx in (1, 3, 2):
                 spread(other, dx, 0)
 
+    value = p_sum(3)
+    p2s[0], p2sc[0] = encode(value)
+    to = (at(0, 1), st)
+    send(p2s.at[0], p2r.at[0], 10, p2sem.at[0], to)
+    send(p2sc.at[0], p2rc.at[0], 11, p2sem.at[1], to)
+
     load_tr.wait()
     load_mask.wait()
 
@@ -191,11 +197,6 @@
     q_second(4)
     q_second(5)
     q_second(6)
-    value = p_sum(3)
-    p2s[0], p2sc[0] = encode(value)
-    to = (at(0, 1), st)
-    send(p2s.at[0], p2r.at[0], 10, p2sem.at[0], to)
-    send(p2sc.at[0], p2rc.at[0], 11, p2sem.at[1], to)
     q_second(7)
 
     owner = x // 2
@@ -209,10 +210,10 @@
         if n > 1:
             arrive(fg.at[who, own], f1sem.at[who])
         src = fg.at[who, own, qcols]
-        dst = fr.at[quarter, tm]
+        dst = fr.at[quarter, zh * 8 + y * 2 + c]
         to = who * 2 + owner
-        cp = pltpu.make_async_remote_copy(src, dst, handsem.at[n], f2sem.at[0], device_id=(to, st), device_id_type=MESH)
-        pl.when(to == tm)(pltpu.make_async_copy(src, dst, f2sem.at[1]).start)
+        cp = pltpu.make_async_remote_copy(src, dst, handsem.at[n], f2sem.at[zh], device_id=(to, st), device_id_type=MESH)
+        pl.when(to == tm)(pltpu.make_async_copy(src, dst, f2sem.at[2]).start)
         pl.when(to != tm)(cp.start)
         handed.append((to, cp))
         part = jnp.dot(fg[who], am[pl.ds(pl.multiple_of(who * 512, 512), 512), :], preferred_element_type=F32)
@@ -256,12 +257,14 @@
 
     @pl.when(mine)
     def _():
-        pltpu.make_async_copy(fr.at[quarter, tm], fr.at[quarter, tm], f2sem.at[1]).wait()
-        arrive(fr.at[quarter, pl.ds(0, 15)], f2sem.at[0])
-        hand_on(quarter, 0, 1, 16).start()
-        hand_on(quarter, 1, 3, 17).start()
-        hand_on(quarter, 1, 1, 18).start()
-        hand_on(quarter, 0, 3, 19).start()
+        near = fr.at[quarter, zh * 8 + y * 2 + c]
+        pltpu.make_async_copy(near, near, f2sem.at[2]).wait()
+        arrive(fr.at[quarter, pl.ds(0, 7)], f2sem.at[zh])
+        hand_on(quarter, zh, 1, 16).start()
+        hand_on(quarter, zh, 3, 17).start()
+        arrive(fr.at[quarter, pl.ds(0, 8)], f2sem.at[1 - zh])
+        hand_on(quarter, 1 - zh, 1, 18).start()
+        hand_on(quarter, 1 - zh, 3, 19).start()
 
     arrive(tot.at[pl.ds(0, 7)], totsem.at[0])
     sums = tot[0]
@@ -306,13 +309,13 @@
 
         @pl.when(away == 1)
         def _(q=q):
-            handed_part(q, 0)
-            hand_on(q, 0, 1, 20).start()
+            handed_part(q, zh)
+            hand_on(q, zh, 1, 20).start()
 
         @pl.when(away == 3)
         def _(q=q):
-            handed_part(q, 1)
-            hand_on(q, 1, 3, 20).start()
+            handed_part(q, 1 - zh)
+            hand_on(q, 1 - zh, 3, 20).start()
 
     for dy in (1, 3, 2):
         who = at(dy, 0)
@@ -336,14 +339,16 @@
         w_send(h, who, 0, 0, 1)
     for q in range(2):
         away = (x + 4 - 2 * c - q) % 4
-        pl.when(jnp.logical_or(away == 2, away == 3))(functools.partial(handed_part, q, 0))
-        pl.when(jnp.logical_or(away == 2, away == 1))(functools.partial(handed_part, q, 1))
-        later = pltpu.roll(fr[q].reshape(16 * rows, 128).astype(F32), 1, 0).reshape(8, 2, rows, 128)
+        pl.when(jnp.logical_or(away == 2, away == 3))(functools.partial(handed_part, q, zh))
+        pl.when(jnp.logical_or(away == 2, away == 1))(functools.partial(handed_part, q, 1 - zh))
+        lies = jnp.concatenate([fr[q, pl.ds(8 * k + 2 * n, 2)].reshape(group, 128) for n in range(4) for k in range(2)], axis=0)
+        later = pltpu.roll(lies.astype(F32), 1, 0).reshape(8, 2, rows, 128)
         for k in range(2):
             lt[k, pl.ds(q * 128, 128), :] = later[:, k].reshape(8 * rows, 128).T.astype(BF16)
     at_rows = pl.ds(pl.multiple_of(tm * 256, 256), 256)
     scale = STATES * STATES / time_total
-    pair = [jnp.dot(lt[c], w[h, c].reshape(8 * rows, half), preferred_element_type=F32) for h in range(2)]
+    for h in range(2):
+        pair[h] = jnp.dot(lt[c], w[h, c].reshape(8 * rows, half), preferred_element_type=F32)
     for h in range(2):
         arrive(w.at[h, 1 - c], coresem.at[h])
         both = pair[h] + jnp.dot(lt[1 - c], w[h, 1 - c].reshape(8 * rows, half), preferred_element_type=F32)
@@ -366,7 +371,7 @@
 
     @pl.when(mine)
     def _():
-        for n, (m, dx) in enumerate(((0, 1), (1, 3), (1, 1), (0, 3))):
+        for n, (m, dx) in enumerate(((zh, 1), (zh, 3), (1 - zh, 1), (1 - zh, 3))):
             hand_on(quarter, m, dx, 16 + n).wait_send()
 
     sent(fr.at[0, pl.ds(0, 8)], 20)
@@ -385,7 +390,7 @@
     dma = pltpu.SemaphoreType.DMA
     scratch = [
         pltpu.SMEM(block_mask.shape, jnp.int32), vm((2, 256, 8 * rows), BF16), vm((8, 2 * rows, neurons), jnp.int32), vm((neurons, width), BF16), vm((rows, width), BF16), vm((rows, width), F32),
-        vm((STATES, width), BF16), vm((STATES, width), BF16), vm((1, width), F32), vm((1, width), F32),
+        vm((STATES, width), BF16), vm((STATES, width), BF16), vm((1, width), F32), vm((1, width), F32), vm((2, 256, 256), F32),
         vm((8, 16 + rows, width), BF16), vm((2, 16, rows, 128), BF16),
         vm((8, rows, width), F32), vm((8, rows, width), F32), vm((8, rows, width), F32),
     ]
@@ -393,7 +398,7 @@
         scratch += [vm((n, rows, 256), I16), vm((n, rows, 256), I16), vm((n, 8, 256), F32), vm((n, 8, 256), F32)]
     scratch += [
         vm((16 + rows, width), F32), vm((256, 128), F32), vm((8, 8, 256), F32), vm((8, 256), F32), vm((8, 256), F32), vm((2, 2, 8, rows, 256), BF16),
-        dma((16,)), dma((21,)), dma((8,)), dma((1,)), dma((8,)), dma((1,)), dma((8,)), dma((2,)), dma((4,)),
+        dma((16,)), dma((21,)), dma((8,)), dma((1,)), dma((8,)), dma((1,)), dma((8,)), dma((3,)), dma((4,)),
         dma((2, 6)), dma((2, 4)), dma((2, 3)), dma((2,)), dma((1,)), dma((1,)), dma((2, 8)), dma((2,)),
     ]
     hbm = pl.BlockSpec(memory_space=pl.ANY)

time: 48.9 us -> 47.2 us (0.965)
  Pallas kernels: 48.2 us -> 46.5 us
    pallas_call x1, Pallas kernels: 47.3 us -> 45.6 us  [shards(): pl.pallas_call(functools.partial(kernel, time_total), out_shape=(vm((256,...]
where the time goes in v4:
time: 47.2 us; the launch traced here: 47.1 us
  Pallas kernels  46.5 us (99%)
  between operations  0.64 us (1%)
    pallas_call x1, Pallas kernels, shards(): pl.pallas_call(functools.partial(kernel, time_total), out_shape=(vm((256,...  45.6 us

profile of v4, /device:TPU:1, one launch (start us, length us, event | category | flops | bytes accessed | tf_op | source)
XLA Modules:
  0.0 47.1 jit_solution(17055715961484072053)
XLA Ops:
  0.6 45.6 %shard_map.95 = (f32[256,512]{1,0:T(8,128)S(1)}, f32[8,256]{1,0:T(8,128)S(1)}) custom-call(s32[2304,2048]{1,0:T(8,128)} %spikes.1, bf16[2048,512]{1,0:T(8,128)(2,1)} %log_rate.1, bf16[144,512]{1,0:T(8,128)(2,1)} %forward.1, f32[144,512]{1,0:T(8,128)} %backward.1, bf16[4096,512]{1,0:T(8,128)(2,1)} %transition.1, f32[1,512]{1,0:T(1,128)} %bitcast.2, ...), custom_call_target="tpu_custom_call" | custom-call | tf_op jit(solution)/shard_map/pallas_call | solution.py:405
  46.3 0.8 %shard_map.96 = (f32[256,512]{1,0:T(8,128)}, f32[144]{0:T(256)}) custom-call(f32[256,512]{1,0:T(8,128)S(1)} %get-tuple-element.4.counts, f32[8,256]{1,0:T(8,128)S(1)} %get-tuple-element.5.loglik), custom_call_target="tpu_custom_call" | custom-call | tf_op jit(solution)/shard_map/pallas_call | solution.py:413

commit v5 on v4

--- a/solution.py
+++ b/solution.py
@@ -21,11 +21,15 @@
 def encode(value):
     most = jnp.maximum(jnp.max(jnp.abs(value), axis=0, keepdims=True), 1e-30)
     coded = (value * (TOP / most) + ROUND) - ROUND
-    return coded.astype(jnp.int32).astype(I16), jnp.broadcast_to(most * (1.0 / TOP), (8, value.shape[1]))
+    unit = most * (1.0 / TOP)
+    first = lax.broadcasted_iota(jnp.int32, (8, 128), 0) == 0
+    packed = jnp.where(first, jnp.broadcast_to(unit[:, 0:128], (8, 128)), jnp.broadcast_to(unit[:, 128:256], (8, 128)))
+    return coded.astype(jnp.int32).astype(I16), packed
 
 
 def decode(coded, scale):
-    return coded.astype(jnp.int32).astype(F32) * scale[0:1, :]
+    unit = jnp.concatenate([scale[0:1, :], scale[1:2, :]], axis=1)
+    return coded.astype(jnp.int32).astype(F32) * unit
 
 
 def kernel(time_total, spikes, log_rate, forward, backward, transition, rate, edge, block_mask,
@@ -395,7 +399,7 @@
         vm((8, rows, width), F32), vm((8, rows, width), F32), vm((8, rows, width), F32),
     ]
     for n in (6, 4, 3, 1):
-        scratch += [vm((n, rows, 256), I16), vm((n, rows, 256), I16), vm((n, 8, 256), F32), vm((n, 8, 256), F32)]
+        scratch += [vm((n, rows, 256), I16), vm((n, rows, 256), I16), vm((n, 8, 128), F32), vm((n, 8, 128), F32)]
     scratch += [
         vm((16 + rows, width), F32), vm((256, 128), F32), vm((8, 8, 256), F32), vm((8, 256), F32), vm((8, 256), F32), vm((2, 2, 8, rows, 256), BF16),
         dma((16,)), dma((21,)), dma((8,)), dma((1,)), dma((8,)), dma((1,)), dma((8,)), dma((3,)), dma((4,)),

time: 47.2 us -> 46.9 us (level)
  no operation moved by 1% of the time
where the time goes in v5:
time: 46.9 us; the launch traced here: 46.8 us
  Pallas kernels  46.2 us (99%)
  between operations  0.64 us (1%)
    pallas_call x1, Pallas kernels, shards(): pl.pallas_call(functools.partial(kernel, time_total), out_shape=(vm((256,...  45.4 us

profile of v5, /device:TPU:1, one launch (start us, length us, event | category | flops | bytes accessed | tf_op | source)
XLA Modules:
  0.0 46.8 jit_solution(10977609405144025431)
XLA Ops:
  0.6 45.4 %shard_map.95 = (f32[256,512]{1,0:T(8,128)S(1)}, f32[8,256]{1,0:T(8,128)S(1)}) custom-call(s32[2304,2048]{1,0:T(8,128)} %spikes.1, bf16[2048,512]{1,0:T(8,128)(2,1)} %log_rate.1, bf16[144,512]{1,0:T(8,128)(2,1)} %forward.1, f32[144,512]{1,0:T(8,128)} %backward.1, bf16[4096,512]{1,0:T(8,128)(2,1)} %transition.1, f32[1,512]{1,0:T(1,128)} %bitcast.2, ...), custom_call_target="tpu_custom_call" | custom-call | tf_op jit(solution)/shard_map/pallas_call | solution.py:409
  46.0 0.8 %shard_map.96 = (f32[256,512]{1,0:T(8,128)}, f32[144]{0:T(256)}) custom-call(f32[256,512]{1,0:T(8,128)S(1)} %get-tuple-element.4.counts, f32[8,256]{1,0:T(8,128)S(1)} %get-tuple-element.5.loglik), custom_call_target="tpu_custom_call" | custom-call | tf_op jit(solution)/shard_map/pallas_call | solution.py:417
